TPU v7x, 32 devices: a whole 2x2x4 slice. The times are simulated.
32 devices in a mesh: pass: 8 (over z, y), blk: 4 (over x, core).
Axes of the slice: x: 2, y: 2, z: 4, core: 2. Of those that a mesh axis runs over, the one named last changes fastest.
Arguments:
- state: float32 [5, 32, 64, 1024], P(None, None, 'blk', 'pass'), as said below
- partner: int32 [8], replicated, may hold values from 0 to 7, as said below
- stencil: int32 [1024], P('pass'), may hold values from 0 to 15
- weight_table: float32 [16], replicated, may hold values from 0 to 1
Outputs:
- next_state: float32 [5, 32, 64, 1024], P(None, None, 'blk', 'pass')
Inputs may be any that keep to these rules, and one draw needn't show every extreme that they name: partner[p] = (p + R) mod 8 for one R of 1 to 7 drawn for each step. `state`: every cell's density lies between 0.6 and 1.6 and its pressure between 0.4 and 1.2.
All inputs are finite; a program needn't handle non-finite values.
Results may differ from a plain program's by a relative error of at most 0.0003.
Values sent between devices are 32-bit elements; how exact they have to be, the bound alone decides.
A program may use at most 64 MiB of HBM per device.

v0:
```python
import functools

import jax
import jax.numpy as jnp
from jax import lax
from jax.experimental import pallas as pl
from jax.experimental.pallas import tpu as pltpu
from jax.sharding import PartitionSpec as P

AXIAL_COEF = 0.4
RADIAL_COEF = 0.3
AROUND_COEF = 0.3
MESH = pl.DeviceIdType.MESH


def basics(q):
    inv = 1.0 / q[0]
    pressure = 0.4 * (q[4] - 0.5 * (q[1] * q[1] + q[2] * q[2] + q[3] * q[3]) * inv)
    square = 1.4 * pressure * inv
    return inv, pressure, square * lax.rsqrt(square)


def flux_of(q, base, d, scale):
    inv, pressure, sound = base
    u = q[d] * (inv * (0.5 * scale))
    part = pressure * (0.5 * scale)
    flux = [c * u for c in q]
    flux[d] = flux[d] + part
    flux[4] = flux[4] + pressure * u
    return flux, jnp.abs(u) + sound * (0.5 * scale)


def between(left, flux_left, reach_left, right, flux_right, reach_right):
    reach = jnp.maximum(reach_left, reach_right)
    return [
        (fl + fr) - reach * (b - a)
        for a, fl, b, fr in zip(left, flux_left, right, flux_right)
    ]


def face(left, right, d, scale):
    fl, rl = flux_of(left, basics(left), d, scale)
    fr, rr = flux_of(right, basics(right), d, scale)
    return between(left, fl, rl, right, fr, rr)


def shifted_diff(q, base, d, axis, keep, scale):
    length = q[0].shape[axis]
    up = lambda x: pltpu.roll(x, length - 1, axis)
    flux, reach = flux_of(q, base, d, scale)
    above = between(q, flux, reach, [up(c) for c in q], [up(c) for c in flux], up(reach))
    above = [jnp.where(keep, c, 0.0) for c in above]
    return [c - pltpu.roll(c, 1, axis) for c in above]


def kernel(
    count, turn, state_in, partner_in, stencil_in, table_in, out, sides_out, lower_out, upper_out,
    state, partner, stencil, table,
    planes, mate_in, gathered, edge_out, edge_in, outer, firsts, lasts, left_in, right_in,
    plane_send, plane_recv, side_send, side_recv, load_sem,
):
    me = lax.axis_index("pass")
    blk = lax.axis_index("blk")
    odd = lax.rem(blk, 2)
    mate = blk + 1 - 2 * odd
    facing = 3 - blk
    ahead, behind = lax.rem(me + 1, count), lax.rem(me + count - 1, count)
    radial, axial, lanes = state.shape[1:]
    interface = jnp.logical_or(blk == 1, blk == 2)
    if turn is None:
        partners = list(range(count))
    else:
        sign = jnp.where(blk == 1, 1, -1)
        partners = [lax.rem(me + sign * (turn + k) + 2 * count, count) for k in range(2)]

    loads = [pltpu.make_async_copy(state_in.at[f], state.at[f], load_sem.at[f]) for f in range(5)]
    loads.append(pltpu.make_async_copy(stencil_in, stencil, load_sem.at[5]))
    loads.append(pltpu.make_async_copy(table_in, table, load_sem.at[6]))
    if turn is None:
        loads.append(pltpu.make_async_copy(partner_in, partner, load_sem.at[7]))
    for load in loads:
        load.start()

    barrier = pltpu.get_barrier_semaphore()
    for device in ((ahead, blk), (behind, blk), (me, mate)):
        pl.semaphore_signal(barrier, inc=1, device_id=device, device_id_type=MESH)

    @pl.when(interface)
    def _():
        for j in partners:
            pl.semaphore_signal(barrier, inc=1, device_id=(j, facing), device_id_type=MESH)

    for f in range(5):
        loads[f].wait()
        planes[0, f] = state[f, :, 0, :]
        planes[1, f] = state[f, :, axial - 1, :]
    plane_lane = lax.broadcasted_iota(jnp.int32, (radial, lanes), 1)

    def plane_copies():
        if turn is None:
            return [
                pltpu.make_async_remote_copy(
                    src_ref=planes.at[odd], dst_ref=gathered.at[me],
                    send_sem=plane_send.at[j], recv_sem=plane_recv.at[me],
                    device_id=(j, facing), device_id_type=MESH,
                )
                for j in partners
            ]
        return [
            pltpu.make_async_remote_copy(
                src_ref=src, dst_ref=dst, send_sem=plane_send.at[k], recv_sem=plane_recv.at[k],
                device_id=(partners[k], facing), device_id_type=MESH,
            )
            for k, (src, dst) in enumerate(
                ((planes.at[odd], gathered.at[0]), (edge_out, edge_in))
            )
        ]

    def side_copy(k, src, dst, device):
        return pltpu.make_async_remote_copy(
            src_ref=src, dst_ref=dst, send_sem=side_send.at[k], recv_sem=side_recv.at[k],
            device_id=device, device_id_type=MESH,
        )

    lane = lax.broadcasted_iota(jnp.int32, (axial, lanes), 1)
    row = lax.broadcasted_iota(jnp.int32, (axial, lanes), 0)

    def pack(r, held):
        place = jnp.logical_or(lane == 2 * r, lane == lax.rem(2 * r - 1 + lanes, lanes))
        return tuple(
            jnp.where(place, pltpu.roll(state[f, r], 2 * r, 1), held[f]) for f in range(5)
        )

    held = lax.fori_loop(
        0, radial, pack, tuple(jnp.ones((axial, lanes), jnp.float32) for _ in range(5)), unroll=8
    )
    even_lane = lax.rem(lane, 2) == 0
    low_lane = lane < lanes // 2

    place = [0, 1, lanes // 2, lanes // 2 + 1, 0]

    def dense(target, cols):
        rolled = [pltpu.roll(c, p, 1) if p else c for c, p in zip(cols, place)]
        target[0] = jnp.where(
            low_lane,
            jnp.where(even_lane, rolled[0], rolled[1]),
            jnp.where(even_lane, rolled[2], rolled[3]),
        )
        target[1] = rolled[4]

    dense(firsts, held)
    dense(lasts, [pltpu.roll(c, 1, 1) for c in held])

    if turn is not None:

        @pl.when(interface)
        def _():
            edge = jnp.zeros((radial, lanes), jnp.float32)
            for f in range(5):
                first = pltpu.roll(planes[0, f], f, 1)
                last = pltpu.roll(planes[1, f], f + 1, 1)
                edge = jnp.where(plane_lane == f, jnp.where(blk == 1, last, first), edge)
            edge_out[...] = edge

    not_last_row = row < axial - 1
    not_last_lane = lane < lanes - 1

    def cells(r):
        return tuple(state[f, r] for f in range(5))

    def step(r, carry):
        q, base, flux, reach, below = carry
        following = cells(jnp.minimum(r + 1, radial - 1))
        base_f = basics(following)
        flux_f, reach_f = flux_of(following, base_f, 2, RADIAL_COEF)
        above = between(q, flux, reach, following, flux_f, reach_f)
        total = [c - (a - b) for c, a, b in zip(q, above, below)]
        part = shifted_diff(q, base, 1, 0, not_last_row, AXIAL_COEF)
        total = [c - a for c, a in zip(total, part)]
        part = shifted_diff(q, base, 3, 1, not_last_lane, AROUND_COEF)
        for f in range(5):
            out[f, r] = total[f] - part[f]
        return following, base_f, tuple(flux_f), reach_f, tuple(above)

    q0 = cells(0)
    base0 = basics(q0)
    flux0, reach0 = flux_of(q0, base0, 2, RADIAL_COEF)
    first = between(q0, flux0, reach0, q0, flux0, reach0)
    carry = (q0, base0, tuple(flux0), reach0, tuple(first))
    carry = lax.fori_loop(0, radial // 8, step, carry, unroll=4)

    @pl.when(interface)
    def _():
        pl.semaphore_wait(barrier, 3 + len(partners))

    @pl.when(jnp.logical_not(interface))
    def _():
        pl.semaphore_wait(barrier, 3)

    to_mate = side_copy(0, planes.at[1 - odd], mate_in, (me, mate))
    to_ahead = side_copy(1, lasts, left_in, (ahead, blk))
    to_behind = side_copy(2, firsts, right_in, (behind, blk))
    to_ahead.start()
    to_behind.start()

    @pl.when(interface)
    def _():
        for copy in plane_copies():
            copy.start()

    to_mate.start()

    lax.fori_loop(radial // 8, radial, step, carry, unroll=4)

    def lower_faces(beside):
        for start in range(0, radial, 8):
            rows = slice(start, start + 8)
            flux = face(
                [beside[f, rows] for f in range(5)], [planes[0, f, rows] for f in range(5)], 1, AXIAL_COEF
            )
            for f in range(5):
                lower_out[f, rows] = flux[f]

    def upper_faces(beside):
        for start in range(0, radial, 8):
            rows = slice(start, start + 8)
            flux = face(
                [planes[1, f, rows] for f in range(5)], [beside[f, rows] for f in range(5)], 1, AXIAL_COEF
            )
            for f in range(5):
                upper_out[f, rows] = flux[f]

    to_mate.wait()

    @pl.when(odd == 0)
    def _():
        upper_faces(mate_in)

    @pl.when(odd == 1)
    def _():
        lower_faces(mate_in)

    to_ahead.wait()
    to_behind.wait()
    left = [
        jnp.where(even_lane, pltpu.roll(left_in[f // 4], (lanes - place[f]) % lanes, 1), held[f])
        for f in range(5)
    ]
    right = [
        jnp.where(even_lane, held[f], pltpu.roll(right_in[f // 4], lanes - 1 - place[f], 1))
        for f in range(5)
    ]
    sides = face(left, right, 3, AROUND_COEF)
    for f in range(5):
        sides_out[f] = jnp.where(even_lane, sides[f], -sides[f])

    for load in loads[5:]:
        load.wait()

    @pl.when(jnp.logical_not(interface))
    def _():
        outer[...] = planes[odd]

    @pl.when(interface)
    def _():
        if turn is None:
            for k in range(count):
                pltpu.make_async_remote_copy(
                    src_ref=planes.at[odd], dst_ref=gathered.at[k],
                    send_sem=plane_send.at[k], recv_sem=plane_recv.at[k],
                    device_id=(k, facing), device_id_type=MESH,
                ).wait()
        else:
            for copy in plane_copies():
                copy.wait()
        weights = jnp.zeros((1, lanes), jnp.float32)
        for k in range(table.shape[0]):
            weights = jnp.where(stencil[...] == k, table[k], weights)
        offset = 0 if turn is not None else lax.rem(partner[me] - me + count, count)

        def ghost(main_at, edge_at, shift, edge_lane):
            for f in range(5):
                main = gathered[0, f] if turn is not None else gathered[main_at, f]
                if turn is not None:
                    edge = pltpu.roll(edge_in[...], (edge_lane - f) % lanes, 1)
                else:
                    edge = pltpu.roll(gathered[edge_at, f], shift, 1)
                beside = jnp.where(plane_lane == edge_lane, edge, pltpu.roll(main, shift, 1))
                outer[f] = weights * main + (1.0 - weights) * beside

        @pl.when(blk == 1)
        def _():
            at = lax.rem(me + offset, count)
            ghost(at, lax.rem(at + 1, count), lanes - 1, lanes - 1)

        @pl.when(blk == 2)
        def _():
            at = lax.rem(me - offset + count, count)
            ghost(at, lax.rem(at + count - 1, count), 1, 0)

    @pl.when(odd == 0)
    def _():
        lower_faces(outer)

    @pl.when(odd == 1)
    def _():
        upper_faces(outer)


def section(turn, state, partner, stencil, weight_table):
    count = lax.axis_size("pass")
    _, radial, axial, lanes = state.shape
    hbm = pl.BlockSpec(memory_space=pltpu.HBM)
    f32 = jnp.float32
    held = count if turn is None else 1
    copies = count if turn is None else 2
    return pl.pallas_call(
        functools.partial(kernel, count, turn),
        out_shape=[
            jax.ShapeDtypeStruct(shape, f32)
            for shape in (state.shape, (5, axial, lanes), (5, radial, lanes), (5, radial, lanes))
        ],
        in_specs=[hbm] * 4,
        out_specs=[pl.BlockSpec(memory_space=pltpu.VMEM)] * 4,
        scratch_shapes=[
            pltpu.VMEM(state.shape, f32),
            pltpu.SMEM(partner.shape, jnp.int32),
            pltpu.VMEM(stencil.shape, jnp.int32),
            pltpu.SMEM(weight_table.shape, f32),
            pltpu.VMEM((2, 5, radial, lanes), f32),
            pltpu.VMEM((5, radial, lanes), f32),
            pltpu.VMEM((held, 5, radial, lanes), f32),
            pltpu.VMEM((radial, lanes), f32),
            pltpu.VMEM((radial, lanes), f32),
            pltpu.VMEM((5, radial, lanes), f32),
            pltpu.VMEM((2, axial, lanes), f32),
            pltpu.VMEM((2, axial, lanes), f32),
            pltpu.VMEM((2, axial, lanes), f32),
            pltpu.VMEM((2, axial, lanes), f32),
            pltpu.SemaphoreType.DMA((copies,)),
            pltpu.SemaphoreType.DMA((copies,)),
            pltpu.SemaphoreType.DMA((3,)),
            pltpu.SemaphoreType.DMA((3,)),
            pltpu.SemaphoreType.DMA((8,)),
        ],
        compiler_params=pltpu.CompilerParams(
            collective_id=turn or 0, has_side_effects=True, vmem_limit_bytes=24 * 1024 * 1024
        ),
        cost_estimate=pl.CostEstimate(
            flops=200 * radial * axial * lanes, bytes_accessed=8 * state.size, transcendentals=0
        ),
    )(state, partner, stencil, weight_table)


def store_kernel(value, sides, lower, upper, out, held, sem):
    _, radial, axial, lanes = value.shape
    lane = lax.broadcasted_iota(jnp.int32, (axial, lanes), 1)
    ends = jnp.logical_or(lane == 0, lane == lanes - 1)
    copies = []
    for start in range(0, radial, 8):
        rows = slice(start, start + 8)
        for f in range(5):
            for r in range(start, start + 8):
                moved = pltpu.roll(sides[f], (lanes - 2 * r) % lanes, 1) if r else sides[f]
                held[f, r] = value[f, r] + jnp.where(ends, moved, 0.0)
            held[f, rows, 0, :] = held[f, rows, 0, :] + lower[f, rows]
            held[f, rows, axial - 1, :] = held[f, rows, axial - 1, :] - upper[f, rows]
            copy = pltpu.make_async_copy(
                held.at[f, pl.ds(start, 8)], out.at[f, pl.ds(start, 8)], sem.at[start // 8, f]
            )
            copy.start()
            copies.append(copy)
    for copy in copies:
        copy.wait()


def store(value, sides, lower, upper):
    return pl.pallas_call(
        store_kernel,
        out_shape=jax.ShapeDtypeStruct(value.shape, value.dtype),
        in_specs=[pl.BlockSpec(memory_space=pltpu.VMEM)] * 4,
        out_specs=pl.BlockSpec(memory_space=pltpu.HBM),
        scratch_shapes=[
            pltpu.VMEM(value.shape, value.dtype),
            pltpu.SemaphoreType.DMA((value.shape[1] // 8, 5)),
        ],
        compiler_params=pltpu.CompilerParams(vmem_limit_bytes=24 * 1024 * 1024),
    )(value, sides, lower, upper)


def shards(state, partner, stencil, weight_table):
    count = lax.axis_size("pass")
    operands = (state, partner, stencil.reshape(1, -1), weight_table)
    if count > 8:
        return store(*section(None, *operands))
    parts = lax.switch(
        partner[0] - 1, [functools.partial(section, k) for k in range(1, count)], *operands
    )
    return store(*parts)


def solution(mesh):
    placed = (P(None, None, "blk", "pass"), P(), P("pass"), P())
    return jax.shard_map(
        shards, mesh=mesh, in_specs=placed, out_specs=P(None, None, "blk", "pass"), check_vma=False
    )
```

profile of v0, /device:TPU:1, one launch (start us, length us, event | category | flops | bytes accessed | tf_op | source)
XLA Modules:
  0.0 13.8 jit_solution(9831689654352622847)
XLA Ops:
  0.7 11.8 %conditional.1 = ((f32[5,32,16,128]{3,2,1,0:T(8,128)S(1)}, f32[5,16,128]{2,1,0:T(8,128)S(1)}, f32[5,32,128]{2,1,0:T(8,128)S(1)}, f32[5,32,128]{2,1,0:T(8,128)S(1)})) conditional(s32[]{:T(128)} %bitcast, (f32[5,32,16,128]{3,2,1,0:T(8,128)}, s32[8]{0:T(128)}, s32[1,128]{1,0:T(1,128)}, f32[16]{0:T(128)}) %tuple.41, ...), branch_computations={%region_0.0_spmd, %region_1.0_spmd, %region_2.0_spmd, %region_3.0_... | conditional | flops 13107200 | bytes 2621448 | solution.py:396
  0.7 11.8 %branch_5_fun.1 = (f32[5,32,16,128]{3,2,1,0:T(8,128)S(1)}, f32[5,16,128]{2,1,0:T(8,128)S(1)}, f32[5,32,128]{2,1,0:T(8,128)S(1)}, f32[5,32,128]{2,1,0:T(8,128)S(1)}) custom-call(f32[5,32,16,128]{3,2,1,0:T(8,128)} %get-tuple-element.81.state_in, s32[8]{0:T(128)} %get-tuple-element.82.partner_in, s32[1,128]{1,0:T(1,128)} %get-tuple-element.83.stencil_in, ...), custom_call_target="tpu_custom_call" | custom-call | flops 13107200 | bytes 2621440 | tf_op jit(solution)/shard_map/cond/branch_5_fun/pallas_call | solution.py:317
  12.5 1.3 %shard_map.46 = f32[5,32,16,128]{3,2,1,0:T(8,128)} custom-call(f32[5,32,16,128]{3,2,1,0:T(8,128)S(1)} %get-tuple-element.93.value, f32[5,16,128]{2,1,0:T(8,128)S(1)} %get-tuple-element.94.sides, f32[5,32,128]{2,1,0:T(8,128)S(1)} %get-tuple-element.95.lower, f32[5,32,128]{2,1,0:T(8,128)S(1)} %get-tuple-element.96.upper), custom_call_target="tpu_custom_call" | custom-call | tf_op jit(solution)/shard_map/pallas_call | solution.py:378
where the time goes:
time: 14.1 us; the launch traced here: 13.8 us
  Pallas kernels  13.1 us (93%)
  between operations  0.66 us (5%)
    pallas_call x1, Pallas kernels, section(): pl.pallas_call(functools.partial(kernel, count, turn), out_shape=[jax.Sha...  11.8 us
    pallas_call x1, Pallas kernels, store(): pl.pallas_call(store_kernel, out_shape=jax.ShapeDtypeStruct(value.shape,...  1.33 us

commit v1 on v0

--- a/solution.py
+++ b/solution.py
@@ -106,14 +106,13 @@
                 )
                 for j in partners
             ]
+        pairs = [(planes.at[odd, f], gathered.at[0, f]) for f in range(5)] + [(edge_out, edge_in)]
         return [
             pltpu.make_async_remote_copy(
                 src_ref=src, dst_ref=dst, send_sem=plane_send.at[k], recv_sem=plane_recv.at[k],
-                device_id=(partners[k], facing), device_id_type=MESH,
+                device_id=(partners[k // 5], facing), device_id_type=MESH,
             )
-            for k, (src, dst) in enumerate(
-                ((planes.at[odd], gathered.at[0]), (edge_out, edge_in))
-            )
+            for k, (src, dst) in enumerate(pairs)
         ]
 
     def side_copy(k, src, dst, device):
@@ -121,6 +120,30 @@
             src_ref=src, dst_ref=dst, send_sem=side_send.at[k], recv_sem=side_recv.at[k],
             device_id=device, device_id_type=MESH,
         )
+
+    @pl.when(interface)
+    def _():
+        pl.semaphore_wait(barrier, 3 + len(partners))
+        copies = plane_copies()
+        for copy in copies if turn is None else copies[:5]:
+            copy.start()
+        if turn is not None:
+            edge = jnp.zeros((radial, lanes), jnp.float32)
+            for f in range(5):
+                first = pltpu.roll(planes[0, f], f, 1)
+                last = pltpu.roll(planes[1, f], f + 1, 1)
+                edge = jnp.where(plane_lane == f, jnp.where(blk == 1, last, first), edge)
+            edge_out[...] = edge
+            copies[5].start()
+
+    @pl.when(jnp.logical_not(interface))
+    def _():
+        pl.semaphore_wait(barrier, 3)
+
+    to_mate = side_copy(0, planes.at[1 - odd], mate_in, (me, mate))
+    to_ahead = side_copy(1, lasts, left_in, (ahead, blk))
+    to_behind = side_copy(2, firsts, right_in, (behind, blk))
+    to_mate.start()
 
     lane = lax.broadcasted_iota(jnp.int32, (axial, lanes), 1)
     row = lax.broadcasted_iota(jnp.int32, (axial, lanes), 0)
@@ -150,17 +173,8 @@
 
     dense(firsts, held)
     dense(lasts, [pltpu.roll(c, 1, 1) for c in held])
-
-    if turn is not None:
-
-        @pl.when(interface)
-        def _():
-            edge = jnp.zeros((radial, lanes), jnp.float32)
-            for f in range(5):
-                first = pltpu.roll(planes[0, f], f, 1)
-                last = pltpu.roll(planes[1, f], f + 1, 1)
-                edge = jnp.where(plane_lane == f, jnp.where(blk == 1, last, first), edge)
-            edge_out[...] = edge
+    to_ahead.start()
+    to_behind.start()
 
     not_last_row = row < axial - 1
     not_last_lane = lane < lanes - 1
@@ -187,30 +201,7 @@
     flux0, reach0 = flux_of(q0, base0, 2, RADIAL_COEF)
     first = between(q0, flux0, reach0, q0, flux0, reach0)
     carry = (q0, base0, tuple(flux0), reach0, tuple(first))
-    carry = lax.fori_loop(0, radial // 8, step, carry, unroll=4)
-
-    @pl.when(interface)
-    def _():
-        pl.semaphore_wait(barrier, 3 + len(partners))
-
-    @pl.when(jnp.logical_not(interface))
-    def _():
-        pl.semaphore_wait(barrier, 3)
-
-    to_mate = side_copy(0, planes.at[1 - odd], mate_in, (me, mate))
-    to_ahead = side_copy(1, lasts, left_in, (ahead, blk))
-    to_behind = side_copy(2, firsts, right_in, (behind, blk))
-    to_ahead.start()
-    to_behind.start()
-
-    @pl.when(interface)
-    def _():
-        for copy in plane_copies():
-            copy.start()
-
-    to_mate.start()
-
-    lax.fori_loop(radial // 8, radial, step, carry, unroll=4)
+    lax.fori_loop(0, radial, step, carry, unroll=4)
 
     def lower_faces(beside):
         for start in range(0, radial, 8):
@@ -313,7 +304,7 @@
     hbm = pl.BlockSpec(memory_space=pltpu.HBM)
     f32 = jnp.float32
     held = count if turn is None else 1
-    copies = count if turn is None else 2
+    copies = count if turn is None else 6
     return pl.pallas_call(
         functools.partial(kernel, count, turn),
         out_shape=[

time: 14.1 us -> 13 us (0.922); the launches traced: 13.8 us -> 13.1 us
  Pallas kernels: 13.1 us -> 12.4 us
    pallas_call x1, Pallas kernels: 11.8 us -> 11.1 us  [section(): pl.pallas_call(functools.partial(kernel, count, turn), out_shape=[jax.Sha...]
where the time goes in v1:
time: 13 us; the launch traced here: 13.1 us
  Pallas kernels  12.4 us (95%)
  between operations  0.66 us (5%)
    pallas_call x1, Pallas kernels, section(): pl.pallas_call(functools.partial(kernel, count, turn), out_shape=[jax.Sha...  11.1 us
    pallas_call x1, Pallas kernels, store(): pl.pallas_call(store_kernel, out_shape=jax.ShapeDtypeStruct(value.shape,...  1.33 us

profile of v1, /device:TPU:1, one launch (start us, length us, event | category | flops | bytes accessed | tf_op | source)
XLA Modules:
  0.0 13.1 jit_solution(17315958943741722134)
XLA Ops:
  0.7 11.1 %conditional.1 = ((f32[5,32,16,128]{3,2,1,0:T(8,128)S(1)}, f32[5,16,128]{2,1,0:T(8,128)S(1)}, f32[5,32,128]{2,1,0:T(8,128)S(1)}, f32[5,32,128]{2,1,0:T(8,128)S(1)})) conditional(s32[]{:T(128)} %bitcast, (f32[5,32,16,128]{3,2,1,0:T(8,128)}, s32[8]{0:T(128)}, s32[1,128]{1,0:T(1,128)}, f32[16]{0:T(128)}) %tuple.41, ...), branch_computations={%region_0.0_spmd, %region_1.0_spmd, %region_2.0_spmd, %region_3.0_... | conditional | flops 13107200 | bytes 2621448 | solution.py:387
  0.7 11.1 %branch_4_fun.1 = (f32[5,32,16,128]{3,2,1,0:T(8,128)S(1)}, f32[5,16,128]{2,1,0:T(8,128)S(1)}, f32[5,32,128]{2,1,0:T(8,128)S(1)}, f32[5,32,128]{2,1,0:T(8,128)S(1)}) custom-call(f32[5,32,16,128]{3,2,1,0:T(8,128)} %get-tuple-element.77.state_in, s32[8]{0:T(128)} %get-tuple-element.78.partner_in, s32[1,128]{1,0:T(1,128)} %get-tuple-element.79.stencil_in, ...), custom_call_target="tpu_custom_call" | custom-call | flops 13107200 | bytes 2621440 | tf_op jit(solution)/shard_map/cond/branch_4_fun/pallas_call | solution.py:308
  11.8 1.3 %shard_map.46 = f32[5,32,16,128]{3,2,1,0:T(8,128)} custom-call(f32[5,32,16,128]{3,2,1,0:T(8,128)S(1)} %get-tuple-element.93.value, f32[5,16,128]{2,1,0:T(8,128)S(1)} %get-tuple-element.94.sides, f32[5,32,128]{2,1,0:T(8,128)S(1)} %get-tuple-element.95.lower, f32[5,32,128]{2,1,0:T(8,128)S(1)} %get-tuple-element.96.upper), custom_call_target="tpu_custom_call" | custom-call | tf_op jit(solution)/shard_map/pallas_call | solution.py:369

commit v2 on v1

--- a/solution.py
+++ b/solution.py
@@ -121,30 +121,6 @@
             device_id=device, device_id_type=MESH,
         )
 
-    @pl.when(interface)
-    def _():
-        pl.semaphore_wait(barrier, 3 + len(partners))
-        copies = plane_copies()
-        for copy in copies if turn is None else copies[:5]:
-            copy.start()
-        if turn is not None:
-            edge = jnp.zeros((radial, lanes), jnp.float32)
-            for f in range(5):
-                first = pltpu.roll(planes[0, f], f, 1)
-                last = pltpu.roll(planes[1, f], f + 1, 1)
-                edge = jnp.where(plane_lane == f, jnp.where(blk == 1, last, first), edge)
-            edge_out[...] = edge
-            copies[5].start()
-
-    @pl.when(jnp.logical_not(interface))
-    def _():
-        pl.semaphore_wait(barrier, 3)
-
-    to_mate = side_copy(0, planes.at[1 - odd], mate_in, (me, mate))
-    to_ahead = side_copy(1, lasts, left_in, (ahead, blk))
-    to_behind = side_copy(2, firsts, right_in, (behind, blk))
-    to_mate.start()
-
     lane = lax.broadcasted_iota(jnp.int32, (axial, lanes), 1)
     row = lax.broadcasted_iota(jnp.int32, (axial, lanes), 0)
 
@@ -173,8 +149,34 @@
 
     dense(firsts, held)
     dense(lasts, [pltpu.roll(c, 1, 1) for c in held])
+
+    if turn is not None:
+
+        @pl.when(interface)
+        def _():
+            edge = jnp.zeros((radial, lanes), jnp.float32)
+            for f in range(5):
+                first = pltpu.roll(planes[0, f], f, 1)
+                last = pltpu.roll(planes[1, f], f + 1, 1)
+                edge = jnp.where(plane_lane == f, jnp.where(blk == 1, last, first), edge)
+            edge_out[...] = edge
+
+    @pl.when(interface)
+    def _():
+        pl.semaphore_wait(barrier, 3 + len(partners))
+        for copy in plane_copies():
+            copy.start()
+
+    @pl.when(jnp.logical_not(interface))
+    def _():
+        pl.semaphore_wait(barrier, 3)
+
+    to_mate = side_copy(0, planes.at[1 - odd], mate_in, (me, mate))
+    to_ahead = side_copy(1, lasts, left_in, (ahead, blk))
+    to_behind = side_copy(2, firsts, right_in, (behind, blk))
     to_ahead.start()
     to_behind.start()
+    to_mate.start()
 
     not_last_row = row < axial - 1
     not_last_lane = lane < lanes - 1

time: 13 us -> 13.8 us (1.062)
  Pallas kernels: 12.4 us -> 13.1 us
    pallas_call x1, Pallas kernels: 11.1 us -> 11.8 us  [section(): pl.pallas_call(functools.partial(kernel, count, turn), out_shape=[jax.Sha...]
where the time goes in v2:
time: 13.8 us
  Pallas kernels  13.1 us (95%)
  between operations  0.66 us (5%)
    pallas_call x1, Pallas kernels, section(): pl.pallas_call(functools.partial(kernel, count, turn), out_shape=[jax.Sha...  11.8 us
    pallas_call x1, Pallas kernels, store(): pl.pallas_call(store_kernel, out_shape=jax.ShapeDtypeStruct(value.shape,...  1.33 us

profile of v2, /device:TPU:1, one launch (start us, length us, event | category | flops | bytes accessed | tf_op | source)
XLA Modules:
  0.0 13.8 jit_solution(17957493397476491835)
XLA Ops:
  0.7 11.8 %conditional.1 = ((f32[5,32,16,128]{3,2,1,0:T(8,128)S(1)}, f32[5,16,128]{2,1,0:T(8,128)S(1)}, f32[5,32,128]{2,1,0:T(8,128)S(1)}, f32[5,32,128]{2,1,0:T(8,128)S(1)})) conditional(s32[]{:T(128)} %bitcast, (f32[5,32,16,128]{3,2,1,0:T(8,128)}, s32[8]{0:T(128)}, s32[1,128]{1,0:T(1,128)}, f32[16]{0:T(128)}) %tuple.41, ...), branch_computations={%region_0.0_spmd, %region_1.0_spmd, %region_2.0_spmd, %region_3.0_... | conditional | flops 13107200 | bytes 2621448 | solution.py:389
  0.7 11.8 %branch_3_fun.1 = (f32[5,32,16,128]{3,2,1,0:T(8,128)S(1)}, f32[5,16,128]{2,1,0:T(8,128)S(1)}, f32[5,32,128]{2,1,0:T(8,128)S(1)}, f32[5,32,128]{2,1,0:T(8,128)S(1)}) custom-call(f32[5,32,16,128]{3,2,1,0:T(8,128)} %get-tuple-element.73.state_in, s32[8]{0:T(128)} %get-tuple-element.74.partner_in, s32[1,128]{1,0:T(1,128)} %get-tuple-element.75.stencil_in, ...), custom_call_target="tpu_custom_call" | custom-call | flops 13107200 | bytes 2621440 | tf_op jit(solution)/shard_map/cond/branch_3_fun/pallas_call | solution.py:310
  12.5 1.3 %shard_map.46 = f32[5,32,16,128]{3,2,1,0:T(8,128)} custom-call(f32[5,32,16,128]{3,2,1,0:T(8,128)S(1)} %get-tuple-element.93.value, f32[5,16,128]{2,1,0:T(8,128)S(1)} %get-tuple-element.94.sides, f32[5,32,128]{2,1,0:T(8,128)S(1)} %get-tuple-element.95.lower, f32[5,32,128]{2,1,0:T(8,128)S(1)} %get-tuple-element.96.upper), custom_call_target="tpu_custom_call" | custom-call | tf_op jit(solution)/shard_map/pallas_call | solution.py:371
